TPU v7x, 32 devices: a whole 2x2x4 slice. The times are simulated.
32 devices in a mesh: dp: 2 (over x), expert: 16 (over z, y, core).
Axes of the slice: x: 2, y: 2, z: 4, core: 2. Of those that a mesh axis runs over, the one named last changes fastest.
Arguments:
- tokens: bfloat16 [2048, 7168], P('expert', 'dp'), may hold values from -6 to 6
- cotangent: bfloat16 [2048, 7168], P('expert', 'dp'), may hold values from -6 to 6
- routes: int32 [2048, 4], P('expert'), may hold values from 0 to 15, all different within a row; in each aligned block of 128 rows (0 to 127, 128 to 255, ...) at most 48 rows name the same one
- combine_weights: float32 [2048, 4], P('expert'), may hold values from 0.2 to 1
- gate_weight: bfloat16 [16, 7168, 1024], P('expert', 'dp'), may hold values from -0.0625 to 0.0625
- up_weight: bfloat16 [16, 7168, 1024], P('expert', 'dp'), may hold values from -0.0625 to 0.0625
- down_weight: bfloat16 [16, 1024, 7168], P('expert', None, 'dp'), may hold values from -0.1875 to 0.1875
Outputs:
- grad_tokens: bfloat16 [2048, 7168], P('expert', 'dp')
- grad_gate: bfloat16 [16, 7168, 1024], P('expert', 'dp')
- grad_up: bfloat16 [16, 7168, 1024], P('expert', 'dp')
- grad_down: bfloat16 [16, 1024, 7168], P('expert', None, 'dp')
Inputs may be any that keep to these rules, and one draw needn't show every extreme that they name: `routes`: each row names 4 different experts. Within each aligned block of 128 tokens no expert is named by more than 48 tokens, and in every draw some block has an expert named by exactly 48 tokens.
All inputs are finite; a program needn't handle non-finite values.
Results may differ from a plain program's by a relative error of at most 0.029.
Values may be sent and summed in bfloat16 or wider, within the bound.
A program may use at most 128 MiB of HBM per device.

v0:
```python
import jax
import jax.numpy as jnp
from jax import lax
from jax.sharding import PartitionSpec as P


def contract(left, right, left_dim, right_dim):
    return lax.dot_general(
        left, right, (((left_dim,), (right_dim,)), ((), ())), preferred_element_type=jnp.float32
    )


def local(tokens, cotangent, routes, combine_weights, gate_weight, up_weight, down_weight):
    experts = lax.axis_size("expert")
    tok_count = routes.shape[0]
    top_count = routes.shape[1]
    width = tokens.shape[1]
    capacity = 3 * tok_count * top_count // (2 * experts)
    flat_routes = routes.reshape(-1)
    onehot = (flat_routes[:, None] == jnp.arange(experts, dtype=jnp.int32)[None, :]).astype(
        jnp.int32
    )
    slot_rank = jnp.sum((jnp.cumsum(onehot, axis=0) - onehot) * onehot, axis=1)
    slots = flat_routes * capacity + slot_rank
    x_pairs = jnp.repeat(tokens, top_count, axis=0)
    scaled = (combine_weights[:, :, None] * cotangent[:, None, :].astype(jnp.float32)).astype(
        jnp.bfloat16
    )
    scaled = scaled.reshape(tok_count * top_count, width)
    empty = jnp.zeros((experts * capacity, width), jnp.bfloat16)
    send_x = empty.at[slots].set(x_pairs).reshape(experts, capacity, width)
    send_s = empty.at[slots].set(scaled).reshape(experts, capacity, width)
    weight_g = gate_weight[0]
    weight_u = up_weight[0]
    weight_d = down_weight[0]
    recv_x, recv_s = (
        lax.all_to_all(send_x, "expert", split_axis=0, concat_axis=0, tiled=True),
        lax.all_to_all(send_s, "expert", split_axis=0, concat_axis=0, tiled=True),
    )
    gate_part = jnp.dot(
        recv_x.reshape(-1, width), weight_g, preferred_element_type=jnp.float32
    ).astype(jnp.bfloat16)
    up_part = jnp.dot(
        recv_x.reshape(-1, width), weight_u, preferred_element_type=jnp.float32
    ).astype(jnp.bfloat16)
    rows_x = recv_x.reshape(-1, width)
    rows_s = recv_s.reshape(-1, width)
    back_part = contract(rows_s, weight_d, 1, 1).astype(jnp.bfloat16)
    gate_share, upper_share = (
        lax.psum_scatter(gate_part, "dp", scatter_dimension=1, tiled=True).astype(jnp.float32),
        lax.psum_scatter(up_part, "dp", scatter_dimension=1, tiled=True).astype(jnp.float32),
    )
    activation = jax.nn.silu(gate_share)
    hidden_share = (activation * upper_share).astype(jnp.bfloat16)
    hidden = lax.all_gather(hidden_share, "dp", axis=1, tiled=True)
    dhidden = lax.psum_scatter(back_part, "dp", scatter_dimension=1, tiled=True).astype(jnp.float32)
    sigmoid_g = jax.nn.sigmoid(gate_share)
    slope = sigmoid_g * (1.0 + gate_share * (1.0 - sigmoid_g))
    gate_grad_share = (dhidden * upper_share * slope).astype(jnp.bfloat16)
    up_grad_share = (dhidden * activation).astype(jnp.bfloat16)
    pre_gate, pre_up = (
        lax.all_gather(gate_grad_share, "dp", axis=1, tiled=True),
        lax.all_gather(up_grad_share, "dp", axis=1, tiled=True),
    )
    back_rows = (contract(pre_gate, weight_g, 1, 1) + contract(pre_up, weight_u, 1, 1)).astype(
        jnp.bfloat16
    )
    returned = lax.all_to_all(
        back_rows.reshape(experts, capacity, width),
        "expert",
        split_axis=0,
        concat_axis=0,
        tiled=True,
    )
    grad_down = contract(hidden, rows_s, 0, 0).astype(jnp.bfloat16)[None]
    grad_gate = contract(rows_x, pre_gate, 0, 0).astype(jnp.bfloat16)[None]
    grad_up = contract(rows_x, pre_up, 0, 0).astype(jnp.bfloat16)[None]
    picked = returned.reshape(experts * capacity, width)[slots]
    grad_tokens = jnp.sum(
        picked.reshape(tok_count, top_count, width).astype(jnp.float32), axis=1
    ).astype(jnp.bfloat16)
    return (grad_tokens, grad_gate, grad_up, grad_down)


def solution(mesh):
    placed = (
        P("expert", "dp"),
        P("expert", "dp"),
        P("expert", None),
        P("expert", None),
        P("expert", "dp", None),
        P("expert", "dp", None),
        P("expert", None, "dp"),
    )
    return jax.shard_map(
        local,
        mesh=mesh,
        in_specs=placed,
        out_specs=(
            P("expert", "dp"),
            P("expert", "dp", None),
            P("expert", "dp", None),
            P("expert", None, "dp"),
        ),
        check_vma=False,
    )
```

profile of v0, /device:TPU:13, one launch (start us, length us, event | category | flops | bytes accessed | tf_op | source)
XLA Modules:
  0.0 553.8 jit_solution(13014328284269601869)
XLA Ops:
  7.2 0.8 copy.12
  8.0 0.1 eq.29
  8.1 0.1 eq.25
  8.2 0.7 broadcast_multiply_fusion
  8.9 1.1 reduce-window.6
  10.0 0.2 slice_reduce_fusion
  10.3 0.1 copy.11
  10.4 0.1 mul.61
  10.5 4.0 broadcast_in_dim.22
  14.5 6.7 %reshape.116 = bf16[512,3584]{1,0:T(8,128)(2,1)} reshape(bf16[128,4,3584]{2,1,0:T(4,128)(2,1)} %broadcast_in_dim.22) | data formatting | bytes 7340032 | tf_op jit(solution)/shard_map/reshape | solution.py:25
  21.2 0.1 fusion.40
  21.3 10.3 %scatter_custom_fusion.1 = bf16[768,3584]{1,0:T(8,128)(2,1)} fusion(s32[512]{0:T(512)S(1)} %bitcast.68, bf16[512,3584]{1,0:T(8,128)(2,1)} %reshape.116, bf16[]{:T(256)} %constant.5.clone.1), kind=kCustom, calls=%fused_computation.23 | custom fusion | bytes 5505536 | tf_op jit(solution)/shard_map/scatter | solution.py:31
  31.6 0.0 copy-start
  31.6 7.3 %all-to-all-start.1 = ((bf16[16,48,3584]{2,1,0:T(8,128)(2,1)}), bf16[16,48,3584]{2,1,0:T(8,128)(2,1)}, u32[]{:S(2)}, u32[]{:S(2)}) async-start(bf16[16,48,3584]{2,1,0:T(8,128)(2,1)} %bitcast.66), calls=%async_computation.2 | async-start | bytes 11010048 | tf_op jit(solution)/shard_map/all_to_all | solution.py:37
  38.9 0.0 copy-done
  38.9 4.0 mul.65
  42.9 0.0 copy-start.1
  42.9 9.0 %mul.66 = f32[512,3584]{1,0:T(8,128)} reshape(f32[128,4,3584]{2,1,0:T(4,128)} %mul.65) | data formatting | bytes 14680064 | tf_op jit(solution)/shard_map/mul | solution.py:26
  51.9 0.0 copy-done.1
  51.9 0.1 copy.15
  52.0 0.1 mul.63
  52.1 11.4 %scatter_custom_fusion = bf16[768,3584]{1,0:T(8,128)(2,1)} fusion(s32[512]{0:T(512)S(1)} %bitcast.69, f32[512,3584]{1,0:T(8,128)} %mul.66, f32[512]{0:T(512)S(1)} %mul.63, bf16[]{:T(256)} %constant.5.clone.1), kind=kCustom, calls=%fused_computation.21 | custom fusion | flops 3670016 | bytes 12847106 | tf_op jit(solution)/shard_map/scatter | solution.py:32
  63.4 95.8 %all-to-all-done.1 = bf16[16,48,3584]{2,1,0:T(8,128)(2,1)} async-done(((bf16[16,48,3584]{2,1,0:T(8,128)(2,1)}), bf16[16,48,3584]{2,1,0:T(8,128)(2,1)}, u32[]{:S(2)}, u32[]{:S(2)}) %all-to-all-start.1) | async-done | bytes 5505056 | tf_op jit(solution)/shard_map/all_to_all | solution.py:37
  159.3 4.9 all-to-all-start
  164.2 0.0 reduce-scatter.6.cloned.1.call-start
  164.2 10.6 %fusion.23 = bf16[768,1024]{1,0:T(8,128)(2,1)} fusion(bf16[768,3584]{1,0:T(8,128)(2,1)} %bitcast.7, bf16[1,3584,1024]{2,1,0:T(8,128)(2,1)} %param.12), kind=kOutput, calls=%fused_computation.33 | convolution fusion | flops 5637931008 | bytes 14417920 | tf_op jit(solution)/shard_map/dot_general | solution.py:43
  174.8 0.0 reduce-scatter.6.cloned.1.call-update
  174.8 0.2 reduce-scatter.8.cloned.1.call-start
  175.0 10.6 %fusion.26 = bf16[768,1024]{1,0:T(8,128)(2,1)} fusion(bf16[768,3584]{1,0:T(8,128)(2,1)} %bitcast.7, bf16[1,3584,1024]{2,1,0:T(8,128)(2,1)} %param.11), kind=kOutput, calls=%fused_computation.34 | convolution fusion | flops 5637931008 | bytes 14417920 | tf_op jit(solution)/shard_map/dot_general | solution.py:40
  185.6 0.0 reduce-scatter.8.cloned.1.call-update
  185.6 0.0 reduce-scatter.4.cloned.1.call-start
  185.7 99.0 %all-to-all-done = bf16[16,48,3584]{2,1,0:T(8,128)(2,1)} async-done(((bf16[16,48,3584]{2,1,0:T(8,128)(2,1)}), bf16[16,48,3584]{2,1,0:T(8,128)(2,1)}, u32[]{:S(2)}, u32[]{:S(2)}) %all-to-all-start) | async-done | bytes 5505056 | tf_op jit(solution)/shard_map/all_to_all | solution.py:38
  284.7 10.6 %fusion.20 = bf16[768,1024]{1,0:T(8,128)(2,1)} fusion(bf16[768,3584]{1,0:T(8,128)(2,1)} %bitcast.4, bf16[1,1024,3584]{2,1,0:T(8,128)(2,1)} %param.13), kind=kOutput, calls=%fused_computation.32 | convolution fusion | flops 5637931008 | bytes 14417920 | tf_op jit(solution)/shard_map/dot_general | solution.py:8
  295.4 0.0 reduce-scatter.4.cloned.1.call-update
  295.4 0.0 all-gather.4.cloned.1.call-start
  295.4 0.0 reduce-scatter.6.cloned.1.call-done
  295.5 0.0 reduce-scatter.8.cloned.1.call-done
  295.5 25.6 %reduce-scatter.4.cloned.1.call-done = bf16[768,512]{1,0:T(8,128)(2,1)} async-done(((bf16[768,1024]{1,0:T(8,128)(2,1)}), bf16[768,512]{1,0:T(8,128)(2,1)}) %reduce-scatter.4.cloned.1.call-update) | async-done | bytes 786448 | tf_op jit(solution)/shard_map/reduce_scatter | solution.py:56
  321.1 4.2 fusion.32
  325.3 0.0 all-gather.4.cloned.1.call-update
  325.3 0.0 all-gather.6.cloned.1.call-start
  325.3 0.5 all-gather.6.cloned.1.call-update
  325.9 26.8 %all-gather.4.cloned.1.call-done = bf16[768,1024]{1,0:T(8,128)(2,1)} async-done(((bf16[768,512]{1,0:T(8,128)(2,1)}), bf16[768,1024]{1,0:T(8,128)(2,1)}) %all-gather.4.cloned.1.call-update) | async-done | bytes 1572880 | tf_op jit(solution)/shard_map/all_gather | solution.py:62
  352.7 11.1 %fusion = f32[768,3584]{1,0:T(8,128)} fusion(bf16[768,1024]{1,0:T(8,128)(2,1)} %all-gather.4.cloned.1.call-done, bf16[1,3584,1024]{2,1,0:T(8,128)(2,1)} %param.11), kind=kOutput, calls=%fused_computation.7 | convolution fusion | flops 5637144576 | bytes 19922944 | tf_op jit(solution)/shard_map/dot_general | solution.py:8
  363.7 18.2 %all-gather.6.cloned.1.call-done = bf16[768,1024]{1,0:T(8,128)(2,1)} async-done(((bf16[768,512]{1,0:T(8,128)(2,1)}), bf16[768,1024]{1,0:T(8,128)(2,1)}) %all-gather.6.cloned.1.call-update) | async-done | bytes 1572880 | tf_op jit(solution)/shard_map/all_gather | solution.py:63
  382.0 11.8 %add_convert_fusion = bf16[768,3584]{1,0:T(8,128)(2,1)} fusion(f32[768,3584]{1,0:T(8,128)} %fusion, bf16[768,1024]{1,0:T(8,128)(2,1)} %all-gather.6.cloned.1.call-done, bf16[1,3584,1024]{2,1,0:T(8,128)(2,1)} %param.12), kind=kOutput, calls=%fused_computation.3 | convolution fusion | flops 5642649600 | bytes 25427968 | tf_op jit(solution)/shard_map/dot_general | solution.py:8
  393.7 6.4 %all-to-all-start.2 = ((bf16[16,48,3584]{2,1,0:T(8,128)(2,1)}), bf16[16,48,3584]{2,1,0:T(8,128)(2,1)}, u32[]{:S(2)}, u32[]{:S(2)}) async-start(bf16[16,48,3584]{2,1,0:T(8,128)(2,1)} %bitcast.67), calls=%async_computation.5 | async-start | bytes 11010048 | tf_op jit(solution)/shard_map/all_to_all | solution.py:68
  400.1 0.2 all-gather.8.cloned.1.call-start
  400.3 0.3 all-gather.8.cloned.1.call-update
  400.7 0.0 copy-start.2
  400.7 29.0 %all-gather.8.cloned.1.call-done = bf16[768,1024]{1,0:T(8,128)(2,1)} async-done(((bf16[768,512]{1,0:T(8,128)(2,1)}), bf16[768,1024]{1,0:T(8,128)(2,1)}) %all-gather.8.cloned.1.call-update) | async-done | bytes 1572880 | tf_op jit(solution)/shard_map/all_gather | solution.py:55
  429.7 10.2 %fusion.14 = bf16[1,1024,3584]{2,1,0:T(8,128)(2,1)} fusion(bf16[768,1024]{1,0:T(8,128)(2,1)} %all-gather.8.cloned.1.call-done, bf16[768,3584]{1,0:T(8,128)(2,1)} %bitcast.4), kind=kOutput, calls=%fused_computation.20 | convolution fusion | flops 5640814592 | bytes 14417920 | tf_op jit(solution)/shard_map/dot_general | solution.py:8
  439.9 0.0 copy-done.2
  439.9 0.0 copy-start.3
  439.9 10.7 %fusion.12 = bf16[1,3584,1024]{2,1,0:T(8,128)(2,1)} fusion(bf16[768,3584]{1,0:T(8,128)(2,1)} %bitcast.7, bf16[768,1024]{1,0:T(8,128)(2,1)S(1)} %copy-done.2), kind=kOutput, calls=%fused_computation.18 | convolution fusion | flops 5640814592 | bytes 14417920 | tf_op jit(solution)/shard_map/dot_general | solution.py:8
  450.6 0.0 copy-done.3
  450.6 10.5 %fusion.13 = bf16[1,3584,1024]{2,1,0:T(8,128)(2,1)} fusion(bf16[768,3584]{1,0:T(8,128)(2,1)} %bitcast.7, bf16[768,1024]{1,0:T(8,128)(2,1)S(1)} %copy-done.3), kind=kOutput, calls=%fused_computation.19 | convolution fusion | flops 5640814592 | bytes 14417920 | tf_op jit(solution)/shard_map/dot_general | solution.py:8
  461.2 59.5 %all-to-all-done.2 = bf16[16,48,3584]{2,1,0:T(8,128)(2,1)} async-done(((bf16[16,48,3584]{2,1,0:T(8,128)(2,1)}), bf16[16,48,3584]{2,1,0:T(8,128)(2,1)}, u32[]{:S(2)}, u32[]{:S(2)}) %all-to-all-start.2) | async-done | bytes 5505056 | tf_op jit(solution)/shard_map/all_to_all | solution.py:68
  520.6 11.5 %gather_fusion = bf16[512,3584]{1,0:T(8,128)(2,1)} fusion(bf16[768,3584]{1,0:T(8,128)(2,1)} %bitcast.11, s32[1024]{0:T(1024)S(1)} %pad_clamp_fusion), kind=kCustom, calls=%fused_computation | custom fusion | bytes 7342080 | tf_op jit(solution)/shard_map/gather | solution.py:78
  532.1 7.0 %reshape.95 = bf16[128,4,3584]{2,1,0:T(4,128)(2,1)} reshape(bf16[512,3584]{1,0:T(8,128)(2,1)} %gather_fusion) | data formatting | bytes 7340032 | tf_op jit(solution)/shard_map/reshape | solution.py:80
  539.1 7.4 %reduce_sum.25 = bf16[128,3584]{1,0:T(8,128)(2,1)} reduce(bf16[128,4,3584]{2,1,0:T(4,128)(2,1)} %reshape.95, bf16[]{:T(256)} %constant.5.clone.1), dimensions={1}, to_apply=%region_8.9 | reduce | flops 1376256 | bytes 4587522 | tf_op jit(solution)/shard_map/reduce_sum | solution.py:79
  (5 shorter events, 0.1 us)
Async XLA Ops:
  31.6 7.3 %copy-start = (bf16[128,3584]{1,0:T(8,128)(2,1)S(1)}, bf16[128,3584]{1,0:T(8,128)(2,1)}, u32[]{:S(2)}) copy-start(bf16[128,3584]{1,0:T(8,128)(2,1)} %param.8) | copy-start | bytes 2752516
  31.6 127.7 %all-to-all-start.1 = ((bf16[16,48,3584]{2,1,0:T(8,128)(2,1)}), bf16[16,48,3584]{2,1,0:T(8,128)(2,1)}, u32[]{:S(2)}, u32[]{:S(2)}) async-start(bf16[16,48,3584]{2,1,0:T(8,128)(2,1)} %bitcast.66), calls=%async_computation.2 | async-start | bytes 11010048 | tf_op jit(solution)/shard_map/all_to_all | solution.py:37
  42.9 9.0 %copy-start.1 = (f32[128,4]{0,1:T(4,128)S(1)}, f32[128,4]{0,1:T(4,128)}, u32[]{:S(2)}) copy-start(f32[128,4]{0,1:T(4,128)} %param.10) | copy-start | bytes 6148
  159.3 125.4 %all-to-all-start = ((bf16[16,48,3584]{2,1,0:T(8,128)(2,1)}), bf16[16,48,3584]{2,1,0:T(8,128)(2,1)}, u32[]{:S(2)}, u32[]{:S(2)}) async-start(bf16[16,48,3584]{2,1,0:T(8,128)(2,1)} %bitcast.65), calls=%async_computation | async-start | bytes 11010048 | tf_op jit(solution)/shard_map/all_to_all | solution.py:38
  164.2 131.3 %reduce-scatter.6.cloned.1.call-start = ((), (), s32[]{:S(2)}) async-start(), calls=%async_computation.7 | async-start | bytes 2359296 | tf_op jit(solution)/shard_map/reduce_scatter | solution.py:51
  174.8 120.7 %reduce-scatter.8.cloned.1.call-start = ((), (), s32[]{:S(2)}) async-start(), calls=%async_computation.8 | async-start | bytes 2359296 | tf_op jit(solution)/shard_map/reduce_scatter | solution.py:50
  185.6 135.4 %reduce-scatter.4.cloned.1.call-start = ((), (), s32[]{:S(2)}) async-start(), calls=%async_computation.6 | async-start | bytes 2359296 | tf_op jit(solution)/shard_map/reduce_scatter | solution.py:56
  295.4 57.3 %all-gather.4.cloned.1.call-start = ((), (), s32[]{:S(2)}) async-start(), calls=%async_computation.9 | async-start | bytes 2359296 | tf_op jit(solution)/shard_map/all_gather | solution.py:62
  325.3 56.7 %all-gather.6.cloned.1.call-start = ((), (), s32[]{:S(2)}) async-start(), calls=%async_computation.10 | async-start | bytes 2359296 | tf_op jit(solution)/shard_map/all_gather | solution.py:63
  393.7 126.9 %all-to-all-start.2 = ((bf16[16,48,3584]{2,1,0:T(8,128)(2,1)}), bf16[16,48,3584]{2,1,0:T(8,128)(2,1)}, u32[]{:S(2)}, u32[]{:S(2)}) async-start(bf16[16,48,3584]{2,1,0:T(8,128)(2,1)} %bitcast.67), calls=%async_computation.5 | async-start | bytes 11010048 | tf_op jit(solution)/shard_map/all_to_all | solution.py:68
  400.1 29.6 %all-gather.8.cloned.1.call-start = ((), (), s32[]{:S(2)}) async-start(), calls=%async_computation.11 | async-start | bytes 2359296 | tf_op jit(solution)/shard_map/all_gather | solution.py:55
  400.7 39.3 %copy-start.2 = (bf16[768,1024]{1,0:T(8,128)(2,1)S(1)}, bf16[768,1024]{1,0:T(8,128)(2,1)}, u32[]{:S(2)}) copy-start(bf16[768,1024]{1,0:T(8,128)(2,1)} %all-gather.4.cloned.1.call-done) | copy-start | bytes 4718596
  439.9 10.7 %copy-start.3 = (bf16[768,1024]{1,0:T(8,128)(2,1)S(1)}, bf16[768,1024]{1,0:T(8,128)(2,1)}, u32[]{:S(2)}) copy-start(bf16[768,1024]{1,0:T(8,128)(2,1)} %all-gather.6.cloned.1.call-done) | copy-start | bytes 4718596
Sparse Core Ops, SparseCore 0:
  174.9 26.6 reduce-scatter.5
  204.5 26.0 reduce-scatter.7
  295.5 25.5 reduce-scatter.3
  325.4 27.2 all-gather.3
  354.7 27.1 all-gather.5
  402.8 26.8 all-gather.7
where the time goes:
time: 562 us; the launch traced here: 554 us
  waiting for transfers between devices  355 us (63%)
  matrix products  86.1 us (15%)
  local copies, waits for them, and re-layouts  54.1 us (10%)
  other arithmetic  25 us (4%)
  starting transfers between devices  19.2 us (3%)
  between operations  14.6 us (3%)
    all_to_all x1, waiting for transfers between devices, local(): lax.all_to_all(send_s, 'expert', split_axis=0, concat_axis=0, tiled=True)  99 us
    all_to_all x1, waiting for transfers between devices, local(): lax.all_to_all(send_x, 'expert', split_axis=0, concat_axis=0, tiled=True)  95.8 us
    dot_general x6, matrix products, contract(): lax.dot_general(left, right, (((left_dim,), (right_dim,)), ((), ())), pre...  64.9 us
    all_to_all x1, waiting for transfers between devices, local(): lax.all_to_all(back_rows.reshape(experts, capacity, width), 'expert', spl...  59.5 us
    all_gather x1, waiting for transfers between devices, local(): hidden = lax.all_gather(hidden_share, 'dp', axis=1, tiled=True)  29 us
    all_gather x1, waiting for transfers between devices, local(): lax.all_gather(gate_grad_share, 'dp', axis=1, tiled=True)  26.8 us
    reduce_scatter x1, waiting for transfers between devices, local(): lax.psum_scatter(back_part, 'dp', scatter_dimension=1, tiled=True)  25.6 us
    all_gather x1, waiting for transfers between devices, local(): lax.all_gather(up_grad_share, 'dp', axis=1, tiled=True)  18.2 us
  transfers between devices with their start and end apart: 9, of which 7 were waited for; matrix products, arithmetic and copies ran while one was open for 18% of the time, Pallas kernels for 0%

commit v1 on v0

v1 whole, which is shorter than its diff:
```python
import jax
import jax.numpy as jnp
from jax import lax
from jax.sharding import PartitionSpec as P

F32 = jnp.float32
BF16 = jnp.bfloat16


def contract(left, right, left_dim, right_dim):
    return lax.dot_general(
        left, right, (((left_dim,), (right_dim,)), ((), ())), preferred_element_type=F32
    )


def batched(left, right, left_dim, right_dim):
    return lax.dot_general(
        left, right, (((left_dim,), (right_dim,)), ((0,), (0,))), preferred_element_type=F32
    )


def local(tokens, cotangent, routes, combine_weights, gate_weight, up_weight, down_weight):
    experts = lax.axis_size("expert")
    shards = lax.axis_size("dp")
    chips = experts // 2
    me = lax.axis_index("expert")
    core = me % 2
    tok_count = routes.shape[0]
    top_count = routes.shape[1]
    width = tokens.shape[1]
    capacity = 3 * tok_count * top_count // (2 * experts)
    rows = chips * capacity
    lanes = [list(range(0, experts, 2)), list(range(1, experts, 2))]
    swap = [(i, i ^ 1) for i in range(experts)]
    weight_g = gate_weight[0]
    weight_u = up_weight[0]
    weight_d = down_weight[0]

    def sibling(value):
        return lax.ppermute(value, "expert", swap)

    def gathered(value):
        own = lax.all_gather(value, "expert", axis_index_groups=lanes, axis=0, tiled=False)
        return own, sibling(own)

    def both_parts(part):
        if shards == 2:
            other = lax.ppermute(part, "dp", [(0, 1), (1, 0)])
            return part.astype(F32) + other.astype(F32)
        return jnp.sum(lax.all_gather(part, "dp").astype(F32), axis=0)

    all_routes = lax.all_gather(routes, "expert", axis=0).reshape(chips, 2, tok_count, top_count)
    all_weights = lax.all_gather(combine_weights, "expert", axis=0).reshape(
        chips, 2, tok_count, top_count
    )
    named = (all_routes == me).astype(F32)
    match = jnp.sum(named, axis=3)
    share = jnp.sum(named * all_weights, axis=3)
    rank = jnp.cumsum(match, axis=2) - match
    places = jnp.arange(capacity, dtype=jnp.int32).astype(F32)
    picks = (match[:, :, None, :] > 0) & (rank[:, :, None, :] == places[None, None, :, None])
    slot_share = jnp.sum(jnp.where(picks, share[:, :, None, :], 0.0), axis=3)
    picks = picks.astype(BF16)

    def side(value, which):
        return lax.dynamic_index_in_dim(value, which, axis=1, keepdims=False)

    pick = (side(picks, core), side(picks, 1 - core))
    factor = (side(slot_share, core), side(slot_share, 1 - core))

    x_blocks = gathered(tokens)
    rows_x = [
        batched(p, x, 2, 1).astype(BF16).reshape(rows, width) for p, x in zip(pick, x_blocks)
    ]
    rows_x = jnp.concatenate(rows_x, axis=0)
    cotangent, _ = lax.optimization_barrier((cotangent, x_blocks[0][0, :8, :128]))
    s_blocks = gathered(cotangent)
    gate_part = jnp.dot(rows_x, weight_g, preferred_element_type=F32).astype(BF16)
    up_part = jnp.dot(rows_x, weight_u, preferred_element_type=F32).astype(BF16)
    gate = both_parts(gate_part)
    upper = both_parts(up_part)
    rows_s = [
        (batched(p, s, 2, 1) * f[:, :, None]).astype(BF16).reshape(rows, width)
        for p, s, f in zip(pick, s_blocks, factor)
    ]
    rows_s = jnp.concatenate(rows_s, axis=0)
    dhidden = both_parts(contract(rows_s, weight_d, 1, 1).astype(BF16))

    activation = jax.nn.silu(gate)
    hidden = (activation * upper).astype(BF16)
    sigmoid_g = jax.nn.sigmoid(gate)
    slope = sigmoid_g * (1.0 + gate * (1.0 - sigmoid_g))
    pre_gate = (dhidden * upper * slope).astype(BF16)
    pre_up = (dhidden * activation).astype(BF16)

    pieces = []
    chunks = 2
    step = width // chunks
    for c in range(chunks):
        cols = slice(c * step, (c + 1) * step)
        back = (
            contract(pre_gate, weight_g[cols], 1, 1) + contract(pre_up, weight_u[cols], 1, 1)
        ).astype(BF16)
        back = back.reshape(2, chips, capacity, step)
        mine = batched(pick[0], back[0], 1, 1).astype(BF16)
        theirs = batched(pick[1], back[1], 1, 1).astype(BF16)
        chip_sum = (mine.astype(F32) + sibling(theirs).astype(F32)).astype(BF16)
        pieces.append(
            lax.psum_scatter(
                chip_sum, "expert", scatter_dimension=0, axis_index_groups=lanes, tiled=False
            )
        )
    grad_tokens = jnp.concatenate(pieces, axis=1)
    grad_down = contract(hidden, rows_s, 0, 0).astype(BF16)[None]
    grad_gate = contract(rows_x, pre_gate, 0, 0).astype(BF16)[None]
    grad_up = contract(rows_x, pre_up, 0, 0).astype(BF16)[None]
    return (grad_tokens, grad_gate, grad_up, grad_down)


def solution(mesh):
    placed = (
        P("expert", "dp"),
        P("expert", "dp"),
        P("expert", None),
        P("expert", None),
        P("expert", "dp", None),
        P("expert", "dp", None),
        P("expert", None, "dp"),
    )
    return jax.shard_map(
        local,
        mesh=mesh,
        in_specs=placed,
        out_specs=(
            P("expert", "dp"),
            P("expert", "dp", None),
            P("expert", "dp", None),
            P("expert", None, "dp"),
        ),
        check_vma=False,
    )
```

time: 562 us -> 602 us (1.071)
  waiting for transfers between devices: 355 us -> 432 us
  local copies, waits for them, and re-layouts: 54.1 us -> 0.98 us
  blocking collectives: 0 us -> 41.1 us
  other arithmetic: 25 us -> 5.68 us
  starting transfers between devices: 19.2 us -> 6.57 us
    all_to_all x3 -> x0, waiting for transfers between devices: 254 us -> none  [the longest x1 99 us: local(): lax.all_to_all(send_s, 'expert', split_axis=0, concat_axis=0, tiled=True)]
    all_gather x3 -> x2, waiting for transfers between devices: 74 us -> 223 us  [gathered(): lax.all_gather(value, 'expert', axis_index_groups=lanes, axis=0, tiled=Fa...]
    ppermute x0 -> x7, waiting for transfers between devices: none -> 93.8 us  [the longest x3 81.7 us: both_parts(): other = lax.ppermute(part, 'dp', [(0, 1), (1, 0)])]
    reduce_scatter x3 -> x2, waiting for transfers between devices: 25.6 us -> 114 us  [local(): lax.psum_scatter(chip_sum, 'expert', scatter_dimension=0, axis_index_grou...]
    all_gather x0 -> x2, blocking collectives: none -> 41.1 us  [the longest x1 22.5 us: local(): lax.all_gather(routes, 'expert', axis=0)]
    all_to_all x3 -> x0, starting transfers between devices: 18.5 us -> none  [the longest x1 7.29 us: local(): lax.all_to_all(send_x, 'expert', split_axis=0, concat_axis=0, tiled=True)]
    dot_general x2 -> x10, matrix products: 21.2 us -> 37.2 us  [the longest x8 22.8 us: batched(): lax.dot_general(left, right, (((left_dim,), (right_dim,)), ((0,), (0,))),...]
    reshape x2 -> x0, local copies, waits for them, and re-layouts: 13.7 us -> none  [the longest x1 6.99 us: local(): picked.reshape(tok_count, top_count, width).astype(jnp.float32)]
  transfers between devices with their start and end apart: 9 -> 11, of which waited for: 7 -> 9; matrix products, arithmetic and copies ran while one was open for 18% -> 14% of each run, Pallas kernels for 0% -> 0%
where the time goes in v1:
time: 602 us; the launch traced here: 591 us
  waiting for transfers between devices  432 us (72%)
  matrix products  90.5 us (15%)
  blocking collectives  41.1 us (7%)
  between operations  14.7 us (2%)
  starting transfers between devices  6.57 us (1%)
    all_gather x2, waiting for transfers between devices, gathered(): lax.all_gather(value, 'expert', axis_index_groups=lanes, axis=0, tiled=Fa...  223 us
    reduce_scatter x2, waiting for transfers between devices, local(): lax.psum_scatter(chip_sum, 'expert', scatter_dimension=0, axis_index_grou...  114 us
    ppermute x3, waiting for transfers between devices, both_parts(): other = lax.ppermute(part, 'dp', [(0, 1), (1, 0)])  81.7 us
    dot_general x8, matrix products, contract(): lax.dot_general(left, right, (((left_dim,), (right_dim,)), ((), ())), pre...  53.3 us
    dot_general x8, matrix products, batched(): lax.dot_general(left, right, (((left_dim,), (right_dim,)), ((0,), (0,))),...  22.8 us
    all_gather x1, blocking collectives, local(): lax.all_gather(routes, 'expert', axis=0)  22.5 us
    all_gather x1, blocking collectives, local(): lax.all_gather(combine_weights, 'expert', axis=0)  18.7 us
    ppermute x4, waiting for transfers between devices, sibling(): return lax.ppermute(value, 'expert', swap)  12.1 us
  transfers between devices with their start and end apart: 11, of which 9 were waited for; matrix products, arithmetic and copies ran while one was open for 14% of the time, Pallas kernels for 0%

profile of v1, /device:TPU:13, one launch (start us, length us, event | category | flops | bytes accessed | tf_op | source)
XLA Modules:
  0.0 591.3 jit_solution(5747027060246261530)
XLA Ops:
  7.2 0.0 all-gather.7.cloned.1.call-start
  7.2 0.7 all-gather.7.cloned.1.call-update
  7.9 0.0 all-gather.9.cloned.1.call-start
  7.9 0.7 all-gather.9.cloned.1.call-update
  8.6 0.0 reduce-scatter.5.cloned.1.call-start
  8.7 111.6 %all-gather.7.cloned.1.call-done = bf16[1024,3584]{1,0:T(8,128)(2,1)} async-done(((bf16[128,3584]{1,0:T(8,128)(2,1)}), bf16[1024,3584]{1,0:T(8,128)(2,1)}) %all-gather.7.cloned.1.call-update) | async-done | bytes 7340048 | tf_op jit(solution)/shard_map/all_gather | solution.py:43
  120.3 1.0 collective-permute-start
  121.3 111.4 %all-gather.9.cloned.1.call-done = bf16[1024,3584]{1,0:T(8,128)(2,1)} async-done(((bf16[128,3584]{1,0:T(8,128)(2,1)}), bf16[1024,3584]{1,0:T(8,128)(2,1)}) %all-gather.9.cloned.1.call-update) | async-done | bytes 7340048 | tf_op jit(solution)/shard_map/all_gather | solution.py:43
  232.7 1.0 collective-permute-start.2
  233.7 22.5 %all-gather = s32[2048,4]{0,1:T(4,128)S(1)} all-gather(s32[128,4]{0,1:T(4,128)} %param.9), channel_id=2, replica_groups=mesh['dp'=2,'expert'=16] {'expert'}, dimensions={0}, use_global_device_ids=true | all-gather | bytes 34816 | tf_op jit(solution)/shard_map/all_gather | solution.py:52
  256.2 18.7 %all-gather.2 = f32[2048,4]{0,1:T(4,128)S(1)} all-gather(f32[128,4]{0,1:T(4,128)} %param.10), channel_id=4, replica_groups=mesh['dp'=2,'expert'=16] {'expert'}, dimensions={0}, use_global_device_ids=true | all-gather | bytes 34816 | tf_op jit(solution)/shard_map/all_gather | solution.py:53
  275.0 0.6 reduce_window_sum.11
  275.6 0.3 select_reduce_fusion
  275.8 0.1 compare_and_fusion
  276.0 0.0 slice-start.1
  276.0 4.4 convolution_convert_fusion.4
  280.4 0.0 copy-start.1
  280.4 0.5 slice-done.1
  280.9 1.1 fusion.9
  282.0 0.0 collective-permute-done
  282.0 0.0 slice-start.3
  282.0 4.8 fusion.10
  286.9 0.0 slice-start.4
  286.9 0.0 slice-start.5
  286.9 5.9 fusion.28
  292.8 1.3 collective-permute-start.1
  294.1 0.0 collective-permute-done.2
  294.1 4.2 convolution_convert_fusion.3
  298.3 0.0 copy-start.3
  298.3 0.0 slice-done.4
  298.4 5.8 fusion.34
  304.2 8.6 %fusion.31 = bf16[768,1024]{1,0:T(8,128)(2,1)S(1)} fusion(bf16[1,3584,1024]{2,1,0:T(8,128)(2,1)} %param.12, bf16[384,3584]{1,0:T(8,128)(2,1)S(1)} %bitcast.102, bf16[384,3584]{1,0:T(8,128)(2,1)S(1)} %bitcast.98), kind=kOutput, calls=%fused_computation.49 | convolution fusion | flops 5648941056 | bytes 14417920 | tf_op jit(solution)/shard_map/dot_general | solution.py:79
  312.9 0.3 collective-permute-start.3
  313.1 1.3 collective-permute-start.4
  314.4 14.3 %collective-permute-done.1 = bf16[768,1024]{1,0:T(8,128)(2,1)S(1)} collective-permute-done((bf16[768,1024]{1,0:T(8,128)(2,1)S(1)}, bf16[768,1024]{1,0:T(8,128)(2,1)S(1)}, u32[]{:S(2)}, u32[]{:S(2)}) %collective-permute-start.1) | collective-permute-done | bytes 1572896 | tf_op jit(solution)/shard_map/ppermute | solution.py:48
  328.7 33.7 %collective-permute-done.3 = bf16[768,1024]{1,0:T(8,128)(2,1)S(1)} collective-permute-done((bf16[768,1024]{1,0:T(8,128)(2,1)S(1)}, bf16[768,1024]{1,0:T(8,128)(2,1)S(1)}, u32[]{:S(2)}, u32[]{:S(2)}) %collective-permute-start.3) | collective-permute-done | bytes 1572896 | tf_op jit(solution)/shard_map/ppermute | solution.py:48
  362.4 33.7 %collective-permute-done.4 = bf16[768,1024]{1,0:T(8,128)(2,1)S(1)} collective-permute-done((bf16[768,1024]{1,0:T(8,128)(2,1)S(1)}, bf16[768,1024]{1,0:T(8,128)(2,1)S(1)}, u32[]{:S(2)}, u32[]{:S(2)}) %collective-permute-start.4) | collective-permute-done | bytes 1572896 | tf_op jit(solution)/shard_map/ppermute | solution.py:48
  396.1 2.5 multiply_convert_fusion.1
  398.7 0.0 slice-start.7
  398.7 3.0 fusion.13
  401.8 3.3 add_convert_fusion.2
  405.1 0.2 fusion.66
  405.3 1.2 convolution_convert_fusion.5
  406.5 1.1 collective-permute-start.6
  407.5 6.0 %collective-permute-done.6 = bf16[8,128,1792]{2,1,0:T(8,128)(2,1)S(1)} collective-permute-done((bf16[8,128,1792]{2,1,0:T(8,128)(2,1)S(1)}, bf16[8,128,1792]{2,1,0:T(8,128)(2,1)S(1)}, u32[]{:S(2)}, u32[]{:S(2)}) %collective-permute-start.6) | collective-permute-done | bytes 3670048 | tf_op jit(solution)/shard_map/ppermute | solution.py:40
  413.6 2.9 add_convert_fusion
  416.5 0.0 reduce-scatter.5.cloned.1.call-update
  416.5 0.0 reduce-scatter.3.cloned.1.call-start
  416.6 5.7 fusion.17
  422.3 5.6 add_convert_fusion.3
  427.9 0.2 fusion.65
  428.1 1.2 convolution_convert_fusion.7
  429.3 0.4 collective-permute-start.5
  429.7 6.0 %collective-permute-done.5 = bf16[8,128,1792]{2,1,0:T(8,128)(2,1)S(1)} collective-permute-done((bf16[8,128,1792]{2,1,0:T(8,128)(2,1)S(1)}, bf16[8,128,1792]{2,1,0:T(8,128)(2,1)S(1)}, u32[]{:S(2)}, u32[]{:S(2)}) %collective-permute-start.5) | collective-permute-done | bytes 3670048 | tf_op jit(solution)/shard_map/ppermute | solution.py:40
  435.8 3.0 add_convert_fusion.1
  438.7 0.0 reduce-scatter.3.cloned.1.call-update
  438.8 0.0 copy-start.2
  438.8 0.0 copy-start.4
  438.8 13.3 %fusion.8 = bf16[1,1024,3584]{2,1,0:T(8,128)(2,1)} fusion(bf16[384,3584]{1,0:T(8,128)(2,1)} %bitcast.96, bf16[384,3584]{1,0:T(8,128)(2,1)S(1)} %bitcast.94, bf16[768,1024]{1,0:T(8,128)(2,1)} %copy-done.7, bf16[768,1024]{1,0:T(8,128)(2,1)} %copy-done.6, bf16[768,1024]{1,0:T(8,128)(2,1)} %copy-done.8, bf16[768,1024]{1,0:T(8,128)(2,1)} %copy-done.5), kind=kOutput, calls=%fused_computation.13 | convolution fusion | flops 5661261824 | bytes 19136512 | tf_op jit(solution)/shard_map/dot_general | solution.py:11
  452.2 8.1 %fusion.7 = bf16[1,3584,1024]{2,1,0:T(8,128)(2,1)} fusion(bf16[768,1024]{1,0:T(8,128)(2,1)S(1)} %copy-done.13, bf16[384,3584]{1,0:T(8,128)(2,1)S(1)} %bitcast.103, bf16[384,3584]{1,0:T(8,128)(2,1)S(1)} %bitcast.99), kind=kOutput, calls=%fused_computation.12 | convolution fusion | flops 5651824640 | bytes 14417920 | tf_op jit(solution)/shard_map/dot_general | solution.py:11
  460.2 8.3 %fusion.6 = bf16[1,3584,1024]{2,1,0:T(8,128)(2,1)} fusion(bf16[768,1024]{1,0:T(8,128)(2,1)S(1)} %copy-done.10, bf16[384,3584]{1,0:T(8,128)(2,1)S(1)} %bitcast.104, bf16[384,3584]{1,0:T(8,128)(2,1)S(1)} %bitcast.100), kind=kOutput, calls=%fused_computation.11 | convolution fusion | flops 5651824640 | bytes 14417920 | tf_op jit(solution)/shard_map/dot_general | solution.py:11
  468.5 29.6 %reduce-scatter.5.cloned.1.call-done = bf16[1,128,1792]{2,1,0:T(8,128)(2,1)} async-done(((bf16[8,128,1792]{2,1,0:T(8,128)(2,1)}), bf16[1,128,1792]{2,1,0:T(8,128)(2,1)}) %reduce-scatter.5.cloned.1.call-update) | async-done | bytes 458768 | tf_op jit(solution)/shard_map/reduce_scatter | solution.py:109
  498.1 84.0 %reduce-scatter.3.cloned.1.call-done = bf16[1,128,1792]{2,1,0:T(8,128)(2,1)} async-done(((bf16[8,128,1792]{2,1,0:T(8,128)(2,1)}), bf16[1,128,1792]{2,1,0:T(8,128)(2,1)}) %reduce-scatter.3.cloned.1.call-update) | async-done | bytes 458768 | tf_op jit(solution)/shard_map/reduce_scatter | solution.py:109
  582.2 2.1 pad_maximum_fusion.6
  (45 shorter events, 0.2 us)
Async XLA Ops:
  7.2 113.1 %all-gather.7.cloned.1.call-start = ((), (), s32[]{:S(2)}) async-start(), calls=%async_computation.4 | async-start | bytes 8257536 | tf_op jit(solution)/shard_map/all_gather | solution.py:43
  7.9 224.8 %all-gather.9.cloned.1.call-start = ((), (), s32[]{:S(2)}) async-start(), calls=%async_computation.5 | async-start | bytes 8257536 | tf_op jit(solution)/shard_map/all_gather | solution.py:43
  8.6 489.5 %reduce-scatter.5.cloned.1.call-start = ((), (), s32[]{:S(2)}) async-start(), calls=%async_computation.3 | async-start | bytes 4128768 | tf_op jit(solution)/shard_map/reduce_scatter | solution.py:109
  120.3 161.8 %collective-permute-start = (bf16[8,128,3584]{2,1,0:T(8,128)(2,1)}, bf16[8,128,3584]{2,1,0:T(8,128)(2,1)}, u32[]{:S(2)}, u32[]{:S(2)}) collective-permute-start(bf16[8,128,3584]{2,1,0:T(8,128)(2,1)} %bitcast.87), channel_id=1, source_target_pairs={{0,1},{1,0},{2,3},{3,2},{4,5},{5,4},{6,7},{7,6},{8,9},{9,8},{10,11... | collective-permute-start | bytes 22020104 | tf_op jit(solution)/shard_map/ppermute | solution.py:40
  232.7 61.5 %collective-permute-start.2 = (bf16[8,128,3584]{2,1,0:T(8,128)(2,1)}, bf16[8,128,3584]{2,1,0:T(8,128)(2,1)}, u32[]{:S(2)}, u32[]{:S(2)}) collective-permute-start(bf16[8,128,3584]{2,1,0:T(8,128)(2,1)} %bitcast.91), channel_id=1, source_target_pairs={{0,1},{1,0},{2,3},{3,2},{4,5},{5,4},{6,7},{7,6},{8,9},{9,8},{10,11... | collective-permute-start | bytes 22020104 | tf_op jit(solution)/shard_map/ppermute | solution.py:40
  275.5 4.9 slice-start
  276.0 4.9 slice-start.1
  280.4 23.8 %copy-start.1 = (bf16[8,48,3584]{2,1,0:T(8,128)(2,1)}, bf16[8,48,3584]{2,1,0:T(8,128)(2,1)S(1)}, u32[]{:S(2)}) copy-start(bf16[8,48,3584]{2,1,0:T(8,128)(2,1)S(1)} %convolution_convert_fusion.4) | copy-start | bytes 8257540
  280.9 6.0 %slice-start.2 = ((s8[7340032]{0:T(1024)(128)(4,1)}), s8[4194304]{0:T(1024)(128)(4,1)S(1)}, s32[]{:S(2)}) async-start(s8[7340032]{0:T(1024)(128)(4,1)} %bitcast.115), calls=%async_computation.8 | async-start | bytes 8388608
  282.0 4.9 slice-start.3
  286.9 5.9 %copy-start = (bf16[8,48,3584]{2,1,0:T(8,128)(2,1)}, bf16[8,48,3584]{2,1,0:T(8,128)(2,1)S(1)}, u32[]{:S(2)}) copy-start(bf16[8,48,3584]{2,1,0:T(8,128)(2,1)S(1)} %fusion.10) | copy-start | bytes 8257540
  286.9 11.5 %slice-start.4 = ((s8[7340032]{0:T(1024)(128)(4,1)}), s8[4194304]{0:T(1024)(128)(4,1)S(1)}, s32[]{:S(2)}) async-start(s8[7340032]{0:T(1024)(128)(4,1)} %bitcast.117), calls=%async_computation.10 | async-start | bytes 8388608
  286.9 11.5 %slice-start.5 = ((s8[7340032]{0:T(1024)(128)(4,1)}), s8[3145728]{0:T(1024)(128)(4,1)S(1)}, s32[]{:S(2)}) async-start(s8[7340032]{0:T(1024)(128)(4,1)} %bitcast.117), calls=%async_computation.11 | async-start | bytes 6291456
  292.8 35.9 %collective-permute-start.1 = (bf16[768,1024]{1,0:T(8,128)(2,1)S(1)}, bf16[768,1024]{1,0:T(8,128)(2,1)S(1)}, u32[]{:S(2)}, u32[]{:S(2)}) collective-permute-start(bf16[768,1024]{1,0:T(8,128)(2,1)S(1)} %fusion.28), channel_id=1, source_target_pairs={{0,16},{16,0},{1,17},{17,1},{2,18},{18,2},{3,19},{19,3},{4,20},{20... | collective-permute-start | bytes 4718600 | tf_op jit(solution)/shard_map/ppermute | solution.py:48
  298.3 5.9 copy-start.3
  304.2 91.9 %copy-start.5 = (bf16[768,1024]{1,0:T(8,128)(2,1)}, bf16[768,1024]{1,0:T(8,128)(2,1)S(1)}, u32[]{:S(2)}) copy-start(bf16[768,1024]{1,0:T(8,128)(2,1)S(1)} %fusion.34) | copy-start | bytes 4718596
  312.9 85.8 %copy-start.6 = (bf16[768,1024]{1,0:T(8,128)(2,1)}, bf16[768,1024]{1,0:T(8,128)(2,1)S(1)}, u32[]{:S(2)}) copy-start(bf16[768,1024]{1,0:T(8,128)(2,1)S(1)} %fusion.31) | copy-start | bytes 4718596
  312.9 49.5 %collective-permute-start.3 = (bf16[768,1024]{1,0:T(8,128)(2,1)S(1)}, bf16[768,1024]{1,0:T(8,128)(2,1)S(1)}, u32[]{:S(2)}, u32[]{:S(2)}) collective-permute-start(bf16[768,1024]{1,0:T(8,128)(2,1)S(1)} %fusion.31), channel_id=1, source_target_pairs={{0,16},{16,0},{1,17},{17,1},{2,18},{18,2},{3,19},{19,3},{4,20},{20... | collective-permute-start | bytes 4718600 | tf_op jit(solution)/shard_map/ppermute | solution.py:48
  313.1 83.0 %collective-permute-start.4 = (bf16[768,1024]{1,0:T(8,128)(2,1)S(1)}, bf16[768,1024]{1,0:T(8,128)(2,1)S(1)}, u32[]{:S(2)}, u32[]{:S(2)}) collective-permute-start(bf16[768,1024]{1,0:T(8,128)(2,1)S(1)} %fusion.34), channel_id=1, source_target_pairs={{0,16},{16,0},{1,17},{17,1},{2,18},{18,2},{3,19},{19,3},{4,20},{20... | collective-permute-start | bytes 4718600 | tf_op jit(solution)/shard_map/ppermute | solution.py:48
  362.4 36.2 %copy-start.7 = (bf16[768,1024]{1,0:T(8,128)(2,1)}, bf16[768,1024]{1,0:T(8,128)(2,1)S(1)}, u32[]{:S(2)}) copy-start(bf16[768,1024]{1,0:T(8,128)(2,1)S(1)} %collective-permute-done.3) | copy-start | bytes 4718596
  396.1 2.5 copy-start.8
  396.1 5.7 slice-start.6
  398.7 3.1 copy-start.9
  398.7 3.1 copy-start.11
  398.7 3.1 slice-start.7
  406.5 7.1 %collective-permute-start.6 = (bf16[8,128,1792]{2,1,0:T(8,128)(2,1)S(1)}, bf16[8,128,1792]{2,1,0:T(8,128)(2,1)S(1)}, u32[]{:S(2)}, u32[]{:S(2)}) collective-permute-start(bf16[8,128,1792]{2,1,0:T(8,128)(2,1)S(1)} %convolution_convert_fusion.5), channel_id=1, source_target_pairs={{0,1},{1,0},{2,3},{3,2},{4,5},{5,4},{6,7},{7,6},{8,9},{9,8},{10,11... | collective-permute-start | bytes 11010056 | tf_op jit(solution)/shard_map/ppermute | solution.py:40
  416.5 165.6 %reduce-scatter.3.cloned.1.call-start = ((), (), s32[]{:S(2)}) async-start(), calls=%async_computation.2 | async-start | bytes 4128768 | tf_op jit(solution)/shard_map/reduce_scatter | solution.py:109
  416.6 5.7 copy-start.12
  429.3 6.5 %collective-permute-start.5 = (bf16[8,128,1792]{2,1,0:T(8,128)(2,1)S(1)}, bf16[8,128,1792]{2,1,0:T(8,128)(2,1)S(1)}, u32[]{:S(2)}, u32[]{:S(2)}) collective-permute-start(bf16[8,128,1792]{2,1,0:T(8,128)(2,1)S(1)} %convolution_convert_fusion.7), channel_id=1, source_target_pairs={{0,1},{1,0},{2,3},{3,2},{4,5},{5,4},{6,7},{7,6},{8,9},{9,8},{10,11... | collective-permute-start | bytes 11010056 | tf_op jit(solution)/shard_map/ppermute | solution.py:40
  438.8 13.4 %copy-start.2 = (bf16[8,48,3584]{2,1,0:T(8,128)(2,1)S(1)}, bf16[8,48,3584]{2,1,0:T(8,128)(2,1)}, u32[]{:S(2)}) copy-start(bf16[8,48,3584]{2,1,0:T(8,128)(2,1)} %copy-done.1) | copy-start | bytes 8257540
  438.8 13.4 %copy-start.4 = (bf16[8,48,3584]{2,1,0:T(8,128)(2,1)S(1)}, bf16[8,48,3584]{2,1,0:T(8,128)(2,1)}, u32[]{:S(2)}) copy-start(bf16[8,48,3584]{2,1,0:T(8,128)(2,1)} %copy-done.3) | copy-start | bytes 8257540
  438.8 13.4 %copy-start.13 = (bf16[768,1024]{1,0:T(8,128)(2,1)S(1)}, bf16[768,1024]{1,0:T(8,128)(2,1)}, u32[]{:S(2)}) copy-start(bf16[768,1024]{1,0:T(8,128)(2,1)} %copy-done.11) | copy-start | bytes 4718596
  452.2 8.1 %copy-start.10 = (bf16[768,1024]{1,0:T(8,128)(2,1)S(1)}, bf16[768,1024]{1,0:T(8,128)(2,1)}, u32[]{:S(2)}) copy-start(bf16[768,1024]{1,0:T(8,128)(2,1)} %copy-done.9) | copy-start | bytes 4718596
Sparse Core Ops, SparseCore 0:
  10.2 110.0 all-gather.6
  122.5 110.1 all-gather.8
  416.6 81.4 reduce-scatter.4
  501.6 80.4 reduce-scatter.2
